TPU v7x, 1024 devices: a whole 8x8x8 slice. The times are simulated.
1024 devices in a mesh: rep: 64 (over x, z_hi, core), tp: 16 (over z_lo, y).
Axes of the slice: x: 8, y: 8, z: 8 (z_hi: 4, z_lo: 2; z = z_hi * 2 + z_lo), core: 2. Of those that a mesh axis runs over, the one named last changes fastest.
Arguments:
- gradients: bfloat16 [64, 2048, 1024], P('rep', 'tp'), parts along dimension 1, may hold values from -5 to 5
- errors: float32 [64, 2048, 1024], P('rep', 'tp'), parts along dimension 1, may hold values from -0.75 to 0.75
- sign_flips: int32 [2048, 1024], P('tp'), parts along dimension 0, may hold values from -1 to 1, as said below
- first_exponents: int32 [2048], P('tp'), parts along dimension 0, may hold values from -11 to -6
- second_exponents: int32 [2048], P('tp'), parts along dimension 0, may hold values from -8 to -3
Outputs:
- err_out: float32 [64, 2048, 1024], P('rep', 'tp'), parts along dimension 1
- update: float32 [2048, 1024], P('tp'), parts along dimension 0
There are 16 independent parts, one for each index of `tp`. A program takes and returns all parts, laid end to end along the dimension named above; each array names one. Nothing has to cross between parts.
Inputs may be any that keep to these rules, and one draw needn't show every extreme that they name: `sign_flips`: every entry is -1 or 1.
All inputs are finite; a program needn't handle non-finite values.
Results may differ from a plain program's by a relative error of at most 0.04.
Values may be sent and summed in bfloat16 or wider, within the bound.
A program may use at most 32 MiB of HBM per device.

v0:
```python
import math

import jax
import jax.numpy as jnp
from jax import lax
from jax.sharding import PartitionSpec as P


def hadamard_matrix(length):
    positions = jnp.arange(length, dtype=jnp.int32)
    anded = positions[:, None] & positions[None, :]
    parity = jnp.zeros(anded.shape, jnp.int32)
    for bit_pos in range(length.bit_length() - 1):
        parity = parity + (anded >> bit_pos & 1)
    parity = parity & 1
    return (1 - 2 * parity).astype(jnp.float32) / math.sqrt(length)


def power_two(exponents):
    shifted = exponents + 16
    result = jnp.ones(exponents.shape, jnp.float32)
    for bit_pos in range(5):
        result = result * jnp.where(
            shifted >> bit_pos & 1 == 1, jnp.float32(2.0**2**bit_pos), jnp.float32(1.0)
        )
    return result * jnp.float32(2.0 ** (-16))


def encode(values, exponents):
    scaled = values * power_two(-exponents)[:, None]
    return jnp.clip(scaled, -448.0, 448.0).astype(jnp.bfloat16)


def per_device(gradients, errors, sign_flips, first_exponents, second_exponents):
    length = gradients.shape[2]
    hadamard = hadamard_matrix(length)
    flips = sign_flips.astype(jnp.float32)
    flipped = gradients[0].astype(jnp.float32) * flips
    rotated = jnp.dot(flipped, hadamard, precision=lax.Precision.HIGHEST) + errors[0]
    first_codes = encode(rotated, first_exponents)
    decoded = first_codes.astype(jnp.float32) * power_two(first_exponents)[:, None]
    err_out = (rotated - decoded)[None]
    owned = first_codes.shape[0] // lax.axis_size("rep")
    first_row = lax.axis_index("rep") * owned
    own_sums = lax.psum_scatter(decoded, "rep", scatter_dimension=0, tiled=True)
    own_exponents = lax.dynamic_slice_in_dim(second_exponents, first_row, owned, 0)
    second_codes = encode(own_sums, own_exponents)
    restored = (
        lax.all_gather(second_codes, "rep", axis=0, tiled=True).astype(jnp.float32)
        * power_two(second_exponents)[:, None]
    )
    update = flips * jnp.dot(restored, hadamard, precision=lax.Precision.HIGHEST)
    return (err_out, update)


def solution(mesh):
    in_specs = (P("rep", "tp", None), P("rep", "tp", None), P("tp", None), P("tp"), P("tp"))
    out_specs = (P("rep", "tp", None), P("tp", None))
    return jax.shard_map(
        per_device, mesh=mesh, in_specs=in_specs, out_specs=out_specs, check_vma=False
    )
```

profile of v0, /device:TPU:1, one launch (start us, length us, event | category | flops | bytes accessed | tf_op | source)
XLA Modules:
  0.0 689.2 jit_solution(3875285180442367922)
XLA Ops:
  7.2 0.0 all-reduce.3.cloned.1.call-start
  7.2 0.7 fusion.30
  7.9 9.6 %convert_multiply_fusion.9 = (f32[128,1024]{1,0:T(8,128)}, f32[1,128,1024]{2,1,0:T(8,128)}) fusion(f32[128]{0:T(128)S(1)} %get-tuple-element.5, f32[128]{0:T(128)S(1)} %get-tuple-element.4, f32[1,128,1024]{2,1,0:T(8,128)} %param.6, s32[128,1024]{1,0:T(8,128)} %param.7, bf16[1,128,1024]{2,1,0:T(8,128)(2,1)} %param.5), kind=kOutput, calls=%fused_computation.8 | convolution fusion | flops 1648623616 | bytes 2360320 | tf_op jit(solution)/shard_map/dot_general | solution.py:39
  17.5 0.0 copy-start.1
  17.5 0.0 all-reduce.3.cloned.1.call-update
  17.5 1.3 dynamic-slice
  19.5 0.0 copy-done.1
  19.5 0.1 fusion.28
  19.6 571.2 %all-reduce.3.cloned.1.call-done = f32[128,1024]{1,0:T(8,128)} async-done(((f32[128,1024]{1,0:T(8,128)}), f32[128,1024]{1,0:T(8,128)}) %all-reduce.3.cloned.1.call-update) | async-done | bytes 524304
  590.8 0.8 fusion.10
  591.7 0.0 copy-start
  591.7 82.4 %all-gather = bf16[64,2,1024]{2,1,0:T(2,128)(2,1)S(1)} all-gather(bf16[1,2,1024]{2,1,0:T(2,128)(2,1)S(1)} %fusion.10), channel_id=1, replica_groups=mesh['rep'=64,'tp'=16] {'rep'}, dimensions={0}, use_global_device_ids=true | all-gather | bytes 266240 | tf_op jit(solution)/shard_map/all_gather | solution.py:49
  674.1 0.1 reshape.13
  674.2 0.0 copy-done
  674.2 8.2 %fusion.3 = f32[128,1024]{1,0:T(8,128)} fusion(f32[128,1024]{1,0:T(8,128)S(1)} %reshape.13, s32[128,1024]{1,0:T(8,128)S(1)} %copy-done, f32[128]{0:T(128)S(1)} %fusion.27), kind=kOutput, calls=%fused_computation.4 | convolution fusion | flops 1647706112 | bytes 1573376 | tf_op jit(solution)/shard_map/dot_general | solution.py:52
  (1 shorter events, 0.0 us)
Async XLA Ops:
  7.2 583.7 %all-reduce.3.cloned.1.call-start = ((), (), s32[]{:S(2)}) async-start(), calls=%async_computation | async-start | bytes 1048576
  17.5 2.1 copy-start.1
  591.7 82.5 %copy-start = (s32[128,1024]{1,0:T(8,128)S(1)}, s32[128,1024]{1,0:T(8,128)}, u32[]{:S(2)}) copy-start(s32[128,1024]{1,0:T(8,128)} %param.7) | copy-start | bytes 1572868
Sparse Core Ops, SparseCore 0:
  17.6 573.1 all-reduce.2
where the time goes:
time: 689 us
  waiting for transfers between devices  571 us (83%)
  blocking collectives  82.4 us (12%)
  matrix products  17.8 us (3%)
  between operations  14.7 us (2%)
    unnamed x2, waiting for transfers between devices  571 us
    all_gather x1, blocking collectives, per_device(): lax.all_gather(second_codes, 'rep', axis=0, tiled=True).astype(jnp.float32)  82.4 us
  transfers between devices with their start and end apart: 1, of which 1 were waited for; matrix products, arithmetic and copies ran while one was open for 0% of the time, Pallas kernels for 0%

commit v1 on v0

v1 whole, which is shorter than its diff:
```python
import jax
import jax.numpy as jnp
from jax import lax
from jax.experimental import pallas as pl
from jax.experimental.pallas import tpu as pltpu
from jax.sharding import PartitionSpec as P

LENGTH = 1024
BLOCKS = 128
HALF = 64
CHIPS = 32
ZS = 4
XS = 8
ROWS = 16
COLS = 128
FACTOR = 256
PARTS = LENGTH // FACTOR


def small_hadamard():
    i = lax.broadcasted_iota(jnp.int32, (FACTOR, FACTOR), 0)
    j = lax.broadcasted_iota(jnp.int32, (FACTOR, FACTOR), 1)
    bits = i & j
    bits = bits ^ (bits >> 4)
    bits = bits ^ (bits >> 2)
    bits = bits ^ (bits >> 1)
    return jnp.where((bits & 1) == 1, -1.0 / 32.0, 1.0 / 32.0).astype(jnp.bfloat16)


def rotate(x, matrix):
    rows = x.shape[0]
    stacked = jnp.concatenate(
        [x[:, part * FACTOR : (part + 1) * FACTOR] for part in range(PARTS)], axis=0
    )
    product = jnp.dot(stacked, matrix, preferred_element_type=jnp.float32)
    a, b, c, d = [product[part * rows : (part + 1) * rows] for part in range(PARTS)]
    ab, amb, cd, cmd = a + b, a - b, c + d, c - d
    return jnp.concatenate([ab + cd, amb + cmd, ab - cd, amb - cmd], axis=1)


def column_of(row):
    square = jnp.broadcast_to(row, (BLOCKS, BLOCKS))
    i = lax.broadcasted_iota(jnp.int32, (BLOCKS, BLOCKS), 0)
    j = lax.broadcasted_iota(jnp.int32, (BLOCKS, BLOCKS), 1)
    column = jnp.sum(jnp.where(i == j, square, 0.0), axis=1, keepdims=True)
    return jnp.broadcast_to(column, (BLOCKS, COLS))


def power_two(exponents):
    return (1 << (exponents + 16)).astype(jnp.float32) * jnp.float32(2.0**-16)


def wide(scale):
    return jnp.concatenate([scale] * (LENGTH // COLS), axis=1)


def kernel(
    g_hbm, e_hbm, f_hbm, exp1, exp2, err_hbm, upd_hbm,
    g, e, f, err, upd, codes, from_sibling, sums, parts, code2, gathered, matrix_ref,
    up1, down1, ratio, up2,
    in_sems, out_sems, core_send, core_recv, a_send, a_recv, b_send, b_recv, c_send, c_recv,
):
    me = lax.axis_index("rep")
    core = lax.rem(me, 2)
    chip = me // 2
    x, z = chip // ZS, lax.rem(chip, ZS)
    sibling = me + 1 - 2 * core

    def half(which):
        return pl.ds(pl.multiple_of(which * HALF, HALF), HALF)

    mine, other = half(core), half(1 - core)

    loads = []
    for at, rows in enumerate((other, mine)):
        for which, (source, target) in enumerate(((g_hbm.at[0], g), (f_hbm, f), (e_hbm.at[0], e))):
            copy = pltpu.make_async_copy(
                source.at[rows, :], target.at[rows, :], in_sems.at[3 * at + which]
            )
            copy.start()
            loads.append(copy)

    def peer(step):
        px = lax.rem(x + step // ZS, XS)
        pz = lax.rem(z + lax.rem(step, ZS), ZS)
        return px, pz, (px * ZS + pz) * 2 + core

    barrier = pltpu.get_barrier_semaphore()
    pl.semaphore_signal(barrier, inc=1, device_id={"rep": sibling}, device_id_type=pl.DeviceIdType.MESH)

    @pl.loop(1, CHIPS)
    def _(step):
        pl.semaphore_signal(
            barrier, inc=1, device_id={"rep": peer(step)[2]}, device_id_type=pl.DeviceIdType.MESH
        )

    s1 = power_two(exp1[...])
    s2 = power_two(exp2[...])
    up1[...] = column_of(s1)
    down1[...] = column_of(power_two(-exp1[...]))
    ratio[...] = column_of(s1 * power_two(-exp2[...]))
    up2[...] = column_of(s2)
    matrix = small_hadamard()
    matrix_ref[...] = matrix

    def first(at, rows):
        for copy in loads[3 * at : 3 * at + 3]:
            copy.wait()
        signs = f[rows, :].astype(jnp.float32)
        flipped = (g[rows, :].astype(jnp.float32) * signs).astype(jnp.bfloat16)
        rotated = rotate(flipped, matrix_ref[...]) + e[rows, :]
        code = jnp.clip(rotated * wide(down1[rows, :]), -448.0, 448.0).astype(jnp.bfloat16)
        err[rows, :] = rotated - code.astype(jnp.float32) * wide(up1[rows, :])
        codes[rows, :] = code

    stores = []

    def store(source, target, rows, sem):
        copy = pltpu.make_async_copy(source.at[rows, :], target.at[rows, :], sem)
        copy.start()
        stores.append(copy)

    first(0, other)
    pl.semaphore_wait(barrier, CHIPS)
    to_sibling = pltpu.make_async_remote_copy(
        src_ref=codes.at[other, :], dst_ref=from_sibling, send_sem=core_send, recv_sem=core_recv,
        device_id={"rep": sibling}, device_id_type=pl.DeviceIdType.MESH,
    )
    to_sibling.start()
    store(err, err_hbm.at[0], other, out_sems.at[0])
    first(1, mine)
    store(err, err_hbm.at[0], mine, out_sems.at[1])
    to_sibling.wait()
    pair = codes[mine, :].astype(jnp.float32) + from_sibling[...].astype(jnp.float32)
    sums[...] = pair.astype(jnp.bfloat16)

    def tile(px, pz, first_row):
        return (
            pl.ds(pl.multiple_of(first_row + pz * ROWS, ROWS), ROWS),
            pl.ds(pl.multiple_of(px * COLS, COLS), COLS),
        )

    @pl.loop(1, CHIPS)
    def _(step):
        px, pz, device = peer(step)
        pltpu.make_async_remote_copy(
            src_ref=sums.at[tile(px, pz, 0)], dst_ref=parts.at[step - 1],
            send_sem=a_send, recv_sem=a_recv,
            device_id={"rep": device}, device_id_type=pl.DeviceIdType.MESH,
        ).start()

    pltpu.make_async_copy(parts, parts, a_recv).wait()
    total = sums[tile(x, z, 0)].astype(jnp.float32)
    for step in range(CHIPS - 1):
        total = total + parts[step].astype(jnp.float32)
    own = tile(x, z, core * HALF)
    own_scale = ratio[own[0], :]
    second = jnp.clip(total * own_scale, -448.0, 448.0).astype(jnp.bfloat16)
    gathered[own] = second

    @pl.loop(1, CHIPS)
    def _(step):
        device = peer(step)[2]
        pltpu.make_async_remote_copy(
            src_ref=gathered.at[own], dst_ref=gathered.at[own],
            send_sem=b_send, recv_sem=b_recv,
            device_id={"rep": device}, device_id_type=pl.DeviceIdType.MESH,
        ).start()

    def last(rows):
        restored = rotate(gathered[rows, :], matrix_ref[...])
        upd[rows, :] = restored * wide(up2[rows, :]) * f[rows, :].astype(jnp.float32)

    pltpu.make_async_copy(parts, parts, b_recv).wait()
    forward = pltpu.make_async_remote_copy(
        src_ref=gathered.at[mine, :], dst_ref=gathered.at[mine, :], send_sem=c_send, recv_sem=c_recv,
        device_id={"rep": sibling}, device_id_type=pl.DeviceIdType.MESH,
    )
    forward.start()
    last(mine)
    store(upd, upd_hbm, mine, out_sems.at[2])
    forward.wait()
    last(other)
    store(upd, upd_hbm, other, out_sems.at[3])
    pltpu.make_async_copy(parts, parts, a_send).wait()
    pltpu.make_async_copy(parts, parts, b_send).wait()
    for copy in stores:
        copy.wait()


def per_device(gradients, errors, sign_flips, first_exponents, second_exponents):
    any_space = pl.BlockSpec(memory_space=pl.ANY)
    vmem = pl.BlockSpec(memory_space=pltpu.VMEM)
    whole = (BLOCKS, LENGTH)
    f32, bf16 = jnp.float32, jnp.bfloat16
    dma = pltpu.SemaphoreType.DMA
    return pl.pallas_call(
        kernel,
        out_shape=(jax.ShapeDtypeStruct((1, *whole), f32), jax.ShapeDtypeStruct(whole, f32)),
        in_specs=[any_space, any_space, any_space, vmem, vmem],
        out_specs=(any_space, any_space),
        scratch_shapes=[
            pltpu.VMEM(whole, bf16), pltpu.VMEM(whole, f32), pltpu.VMEM(whole, jnp.int32),
            pltpu.VMEM(whole, f32), pltpu.VMEM(whole, f32),
            pltpu.VMEM(whole, bf16), pltpu.VMEM((HALF, LENGTH), bf16), pltpu.VMEM((HALF, LENGTH), bf16),
            pltpu.VMEM((CHIPS - 1, ROWS, COLS), bf16), pltpu.VMEM((ROWS, COLS), bf16),
            pltpu.VMEM(whole, bf16), pltpu.VMEM((FACTOR, FACTOR), bf16),
            pltpu.VMEM((BLOCKS, COLS), f32), pltpu.VMEM((BLOCKS, COLS), f32),
            pltpu.VMEM((BLOCKS, COLS), f32), pltpu.VMEM((BLOCKS, COLS), f32),
            dma((6,)), dma((4,)), dma, dma, dma, dma, dma, dma, dma, dma,
        ],
        compiler_params=pltpu.CompilerParams(
            collective_id=0, has_side_effects=True, vmem_limit_bytes=60 * 2**20
        ),
    )(
        gradients, errors, sign_flips,
        first_exponents.reshape(1, BLOCKS), second_exponents.reshape(1, BLOCKS),
    )


def solution(mesh):
    in_specs = (P("rep", "tp", None), P("rep", "tp", None), P("tp", None), P("tp"), P("tp"))
    out_specs = (P("rep", "tp", None), P("tp", None))
    return jax.shard_map(
        per_device, mesh=mesh, in_specs=in_specs, out_specs=out_specs, check_vma=False
    )
```

time: 689 us -> 46.3 us (0.07)
  waiting for transfers between devices: 571 us -> 0 us
  blocking collectives: 82.4 us -> 0 us
  Pallas kernels: 0 us -> 42.7 us
  matrix products: 17.8 us -> 0 us
  between operations: 14.7 us -> 0.65 us
    unnamed x2 -> x0, waiting for transfers between devices: 571 us -> none
    all_gather x1 -> x0, blocking collectives: 82.4 us -> none  [per_device(): lax.all_gather(second_codes, 'rep', axis=0, tiled=True).astype(jnp.float32)]
    pallas_call x0 -> x1, Pallas kernels: none -> 42.7 us  [per_device(): pl.pallas_call(kernel, out_shape=(jax.ShapeDtypeStruct((1, *whole), f32),...]
    dot_general x2 -> x0, matrix products: 17.8 us -> none  [the longest x1 9.59 us: per_device(): jnp.dot(flipped, hadamard, precision=lax.Precision.HIGHEST) + errors[0]]
  transfers between devices with their start and end apart: 1 -> 0, of which waited for: 1 -> 0; matrix products, arithmetic and copies ran while one was open for 0% -> 0% of each run, Pallas kernels for 0% -> 0%
where the time goes in v1:
time: 46.3 us; the launch traced here: 46.1 us
  Pallas kernels  42.7 us (92%)
  local copies, waits for them, and re-layouts  2.74 us (6%)
  between operations  0.65 us (1%)
    pallas_call x1, Pallas kernels, per_device(): pl.pallas_call(kernel, out_shape=(jax.ShapeDtypeStruct((1, *whole), f32),...  42.7 us
    unnamed x4, local copies, waits for them, and re-layouts  2.74 us

profile of v1, /device:TPU:1, one launch (start us, length us, event | category | flops | bytes accessed | tf_op | source)
XLA Modules:
  0.0 46.1 jit_solution(6541321073550950648)
XLA Ops:
  0.6 42.7 %shard_map.68 = (f32[1,128,1024]{2,1,0:T(8,128)}, f32[128,1024]{1,0:T(8,128)}) custom-call(bf16[1,128,1024]{2,1,0:T(8,128)(2,1)} %g_hbm.1, f32[1,128,1024]{2,1,0:T(8,128)} %e_hbm.1, s32[128,1024]{1,0:T(8,128)} %f_hbm.1, s32[1,128]{1,0:T(1,128)} %bitcast.2, s32[1,128]{1,0:T(1,128)} %bitcast.3), custom_call_target="tpu_custom_call" | custom-call | tf_op jit(solution)/shard_map/pallas_call | solution.py:197
  43.4 0.0 copy-start
  43.4 1.9 %copy.9 = f32[1,128,1024]{2,1,0:T(8,128)} copy(f32[1,128,1024]{2,1,0:T(8,128)} %get-tuple-element.4) | data formatting | bytes 1048576
  45.3 0.0 copy-done
  45.3 0.8 %copy.10 = f32[128,1024]{1,0:T(8,128)} copy(f32[128,1024]{1,0:T(8,128)S(1)} %copy-done) | data formatting | bytes 1048576
Async XLA Ops:
  43.4 2.0 %copy-start = (f32[128,1024]{1,0:T(8,128)S(1)}, f32[128,1024]{1,0:T(8,128)}, u32[]{:S(2)}) copy-start(f32[128,1024]{1,0:T(8,128)} %get-tuple-element.5) | copy-start | bytes 1572868

commit v2 on v1

v2 whole, which is shorter than its diff:
```python
import jax
import jax.numpy as jnp
from jax import lax
from jax.experimental import pallas as pl
from jax.experimental.pallas import tpu as pltpu
from jax.sharding import PartitionSpec as P

LENGTH = 1024
BLOCKS = 128
HALF = 64
XS = 8
ZS = 4
ROWS = 16
COLS = 512
LANES = 128
FACTOR = 256
PARTS = LENGTH // FACTOR
MESH = pl.DeviceIdType.MESH
FAR_FIRST = (4, 3, 5, 2, 6, 1, 7)
NEAR_FIRST = (1, 7, 2, 6, 3, 5, 4)


def small_hadamard():
    i = lax.broadcasted_iota(jnp.int32, (FACTOR, FACTOR), 0)
    j = lax.broadcasted_iota(jnp.int32, (FACTOR, FACTOR), 1)
    bits = i & j
    bits = bits ^ (bits >> 4)
    bits = bits ^ (bits >> 2)
    bits = bits ^ (bits >> 1)
    return jnp.where((bits & 1) == 1, -1.0 / 32.0, 1.0 / 32.0).astype(jnp.bfloat16)


def rotate(x, matrix):
    rows = x.shape[0]
    stacked = jnp.concatenate(
        [x[:, part * FACTOR : (part + 1) * FACTOR] for part in range(PARTS)], axis=0
    )
    product = jnp.dot(stacked, matrix, preferred_element_type=jnp.float32)
    a, b, c, d = [product[part * rows : (part + 1) * rows] for part in range(PARTS)]
    ab, amb, cd, cmd = a + b, a - b, c + d, c - d
    return jnp.concatenate([ab + cd, amb + cmd, ab - cd, amb - cmd], axis=1)


def column_of(row):
    square = jnp.broadcast_to(row, (BLOCKS, BLOCKS))
    i = lax.broadcasted_iota(jnp.int32, (BLOCKS, BLOCKS), 0)
    j = lax.broadcasted_iota(jnp.int32, (BLOCKS, BLOCKS), 1)
    column = jnp.sum(jnp.where(i == j, square, 0.0), axis=1, keepdims=True)
    return jnp.broadcast_to(column, (BLOCKS, LANES))


def power_two(exponents):
    return (1 << (exponents + 16)).astype(jnp.float32) * jnp.float32(2.0**-16)


def wide(scale, columns):
    return jnp.concatenate([scale] * (columns // LANES), axis=1)


def reduce_kernel(
    g_hbm, e_hbm, f_hbm, exp1_hbm, exp2_hbm, gathered, err, f, matrix, up2,
    g, e, codes, from_sibling, sums, parts, exp1, exp2, up1, down1, ratio,
    exp_sems, in_sems, pair_send, pair_recv, a_send, a_recv, z_send, z_recv, x_send, x_recv, c_send, c_recv,
):
    me = lax.axis_index("rep")
    core = lax.rem(me, 2)
    chip = me // 2
    x, z = chip // ZS, lax.rem(chip, ZS)
    sibling = me + 1 - 2 * core

    def device(px, pz):
        return {"rep": (px * ZS + pz) * 2 + core}

    def turned(step):
        return lax.rem(x + step, XS)

    def half(which):
        return pl.ds(pl.multiple_of(which * HALF, HALF), HALF)

    mine, other = half(core), half(1 - core)

    def slab(px, first_row):
        return (
            pl.ds(pl.multiple_of(first_row + (px // 2) * ROWS, ROWS), ROWS),
            pl.ds(pl.multiple_of(lax.rem(px, 2) * COLS, COLS), COLS),
        )

    small_loads = [
        pltpu.make_async_copy(exp1_hbm, exp1, exp_sems.at[0]),
        pltpu.make_async_copy(exp2_hbm, exp2, exp_sems.at[1]),
    ]
    for copy in small_loads:
        copy.start()
    loads = []
    for at, rows in enumerate((other, mine)):
        for which, (source, target) in enumerate(((g_hbm.at[0], g), (f_hbm, f), (e_hbm.at[0], e))):
            copy = pltpu.make_async_copy(
                source.at[rows, :], target.at[rows, :], in_sems.at[3 * at + which]
            )
            copy.start()
            loads.append(copy)

    barrier = pltpu.get_barrier_semaphore()
    pl.semaphore_signal(barrier, inc=1, device_id={"rep": sibling}, device_id_type=MESH)

    @pl.when(z == 0)
    def _():
        @pl.loop(1, XS * ZS)
        def _(step):
            pl.semaphore_signal(
                barrier, inc=1,
                device_id=device(turned(lax.rem(step, XS)), lax.rem(z + step // XS, ZS)),
                device_id_type=MESH,
            )

    matrix[...] = small_hadamard()
    for copy in small_loads:
        copy.wait()
    s1 = power_two(exp1[...])
    up1[...] = column_of(s1)
    down1[...] = column_of(power_two(-exp1[...]))
    ratio[...] = column_of(s1 * power_two(-exp2[...]))
    up2[...] = column_of(power_two(exp2[...]))

    def first(at, rows):
        for copy in loads[3 * at : 3 * at + 3]:
            copy.wait()
        signs = f[rows, :].astype(jnp.float32)
        flipped = (g[rows, :].astype(jnp.float32) * signs).astype(jnp.bfloat16)
        rotated = rotate(flipped, matrix[...]) + e[rows, :]
        code = jnp.clip(rotated * wide(down1[rows, :], LENGTH), -448.0, 448.0).astype(jnp.bfloat16)
        err[rows, :] = rotated - code.astype(jnp.float32) * wide(up1[rows, :], LENGTH)
        codes[rows, :] = code

    first(0, other)
    pl.semaphore_wait(barrier, jnp.where(z == 0, XS, XS + 1))
    to_sibling = pltpu.make_async_remote_copy(
        src_ref=codes.at[other, :], dst_ref=from_sibling, send_sem=pair_send, recv_sem=pair_recv,
        device_id={"rep": sibling}, device_id_type=MESH,
    )
    to_sibling.start()
    first(1, mine)
    to_sibling.wait()
    pair = codes[mine, :].astype(jnp.float32) + from_sibling[...].astype(jnp.float32)
    sums[...] = pair.astype(jnp.bfloat16)

    def to_owner(px):
        pltpu.make_async_remote_copy(
            src_ref=sums.at[slab(px, 0)], dst_ref=parts.at[z, x],
            send_sem=a_send, recv_sem=a_recv.at[z],
            device_id=device(px, 0), device_id_type=MESH,
        ).start()

    for step in FAR_FIRST:
        to_owner(turned(step))

    @pl.when(z != 0)
    def _():
        to_owner(x)

    own = slab(x, core * HALF)

    def to_relay(pz):
        pltpu.make_async_remote_copy(
            src_ref=gathered.at[own], dst_ref=gathered.at[own],
            send_sem=z_send, recv_sem=z_recv,
            device_id=device(x, pz), device_id_type=MESH,
        ).start()

    def to_row(px):
        pltpu.make_async_remote_copy(
            src_ref=gathered.at[own], dst_ref=gathered.at[own],
            send_sem=x_send, recv_sem=x_recv.at[x],
            device_id=device(px, z), device_id_type=MESH,
        ).start()

    @pl.when(z == 0)
    def _():
        parts[0, x] = sums[slab(x, 0)]
        total = jnp.zeros((ROWS, COLS), jnp.float32)
        for plane in range(ZS):
            landed = parts.at[plane] if plane else parts.at[0, pl.ds(0, XS - 1)]
            pltpu.make_async_copy(landed, landed, a_recv.at[plane]).wait()
            for column in range(XS):
                total = total + parts[plane, column].astype(jnp.float32)
        scaled = total * wide(ratio[own[0], :], COLS)
        gathered[own] = jnp.clip(scaled, -448.0, 448.0).astype(jnp.bfloat16)
        to_relay(1)
        for step in FAR_FIRST:
            to_row(turned(step))
        to_relay(2)
        to_relay(3)

    @pl.when(z != 0)
    def _():
        pltpu.make_async_copy(gathered.at[own], gathered.at[own], z_recv).wait()
        for step in FAR_FIRST:
            to_row(turned(step))

    def to_other_core(px):
        rows = slab(px, core * HALF)
        pltpu.make_async_remote_copy(
            src_ref=gathered.at[rows], dst_ref=gathered.at[rows],
            send_sem=c_send, recv_sem=c_recv,
            device_id={"rep": sibling}, device_id_type=MESH,
        ).start()

    to_other_core(x)
    for step in NEAR_FIRST:
        px = turned(step)
        rows = slab(px, core * HALF)
        pltpu.make_async_copy(gathered.at[rows], gathered.at[rows], x_recv.at[px]).wait()
        to_other_core(px)

    seven = parts.at[0, pl.ds(0, XS - 1)]
    pltpu.make_async_copy(seven, seven, x_send).wait()
    pltpu.make_async_copy(parts.at[0], parts.at[0], c_send).wait()

    @pl.when(z == 0)
    def _():
        three = parts.at[0, pl.ds(0, ZS - 1)]
        pltpu.make_async_copy(seven, seven, a_send).wait()
        pltpu.make_async_copy(three, three, z_send).wait()

    @pl.when(z != 0)
    def _():
        pltpu.make_async_copy(parts.at[0], parts.at[0], a_send).wait()

    pltpu.make_async_copy(parts.at[0], parts.at[0], c_recv).wait()


def update_kernel(gathered, err, f, matrix, up2, err_hbm, upd_hbm, upd, out_sems):
    stores = [pltpu.make_async_copy(err, err_hbm.at[0], out_sems.at[0])]
    stores[0].start()
    for at in range(2):
        rows = pl.ds(at * HALF, HALF)
        restored = rotate(gathered[rows, :], matrix[...]) * wide(up2[rows, :], LENGTH)
        upd[rows, :] = restored * f[rows, :].astype(jnp.float32)
        stores.append(
            pltpu.make_async_copy(upd.at[rows, :], upd_hbm.at[rows, :], out_sems.at[1 + at])
        )
        stores[-1].start()
    for copy in stores:
        copy.wait()


def per_device(gradients, errors, sign_flips, first_exponents, second_exponents):
    hbm = pl.BlockSpec(memory_space=pl.ANY)
    vmem = pl.BlockSpec(memory_space=pltpu.VMEM)
    whole = (BLOCKS, LENGTH)
    f32, bf16, i32 = jnp.float32, jnp.bfloat16, jnp.int32
    dma = pltpu.SemaphoreType.DMA
    arguments = (
        gradients, errors, sign_flips,
        first_exponents.reshape(1, BLOCKS), second_exponents.reshape(1, BLOCKS),
    )
    held = pl.pallas_call(
        reduce_kernel,
        out_shape=(
            pltpu.VMEM(whole, bf16), pltpu.VMEM(whole, f32), pltpu.VMEM(whole, i32),
            pltpu.VMEM((FACTOR, FACTOR), bf16), pltpu.VMEM((BLOCKS, LANES), f32),
        ),
        in_specs=[hbm] * 5,
        out_specs=(vmem,) * 5,
        scratch_shapes=[
            pltpu.VMEM(whole, bf16), pltpu.VMEM(whole, f32),
            pltpu.VMEM(whole, bf16), pltpu.VMEM((HALF, LENGTH), bf16), pltpu.VMEM((HALF, LENGTH), bf16),
            pltpu.VMEM((ZS, XS, ROWS, COLS), bf16),
            pltpu.VMEM((1, BLOCKS), i32), pltpu.VMEM((1, BLOCKS), i32),
            pltpu.VMEM((BLOCKS, LANES), f32), pltpu.VMEM((BLOCKS, LANES), f32),
            pltpu.VMEM((BLOCKS, LANES), f32),
            dma((2,)), dma((6,)), dma, dma, dma, dma((ZS,)), dma, dma, dma, dma((XS,)), dma, dma,
        ],
        compiler_params=pltpu.CompilerParams(
            collective_id=0, has_side_effects=True, vmem_limit_bytes=16 * 2**20
        ),
    )(*[pltpu.with_memory_space_constraint(array, pltpu.HBM) for array in arguments])
    return pl.pallas_call(
        update_kernel,
        out_shape=(jax.ShapeDtypeStruct((1, *whole), f32), jax.ShapeDtypeStruct(whole, f32)),
        in_specs=[vmem] * 5,
        out_specs=(hbm, hbm),
        scratch_shapes=[pltpu.VMEM(whole, f32), dma((3,))],
        compiler_params=pltpu.CompilerParams(vmem_limit_bytes=16 * 2**20),
    )(*held)


def solution(mesh):
    in_specs = (P("rep", "tp", None), P("rep", "tp", None), P("tp", None), P("tp"), P("tp"))
    out_specs = (P("rep", "tp", None), P("tp", None))
    return jax.shard_map(
        per_device, mesh=mesh, in_specs=in_specs, out_specs=out_specs, check_vma=False
    )
```

time: 46.3 us -> 39.9 us (0.86)
  Pallas kernels: 42.7 us -> 39.1 us
  local copies, waits for them, and re-layouts: 2.74 us -> 0 us
    pallas_call x1 -> x2, Pallas kernels: 42.7 us -> 39.1 us  [the longest x1 37.9 us: per_device(): pl.pallas_call(reduce_kernel, out_shape=(pltpu.VMEM(whole, bf16), pltpu.V...]
    unnamed x4 -> x0, local copies, waits for them, and re-layouts: 2.74 us -> none
where the time goes in v2:
time: 39.9 us; the launch traced here: 39.7 us
  Pallas kernels  39.1 us (98%)
  between operations  0.64 us (2%)
    pallas_call x1, Pallas kernels, per_device(): pl.pallas_call(reduce_kernel, out_shape=(pltpu.VMEM(whole, bf16), pltpu.V...  37.9 us
    pallas_call x1, Pallas kernels, per_device(): pl.pallas_call(update_kernel, out_shape=(jax.ShapeDtypeStruct((1, *whole)...  1.13 us

profile of v2, /device:TPU:1, one launch (start us, length us, event | category | flops | bytes accessed | tf_op | source)
XLA Modules:
  0.0 39.7 jit_solution(18347214022552152059)
XLA Ops:
  0.6 37.9 %shard_map.68 = (bf16[128,1024]{1,0:T(8,128)(2,1)S(1)}, f32[128,1024]{1,0:T(8,128)S(1)}, s32[128,1024]{1,0:T(8,128)S(1)}, bf16[256,256]{1,0:T(8,128)(2,1)S(1)}, f32[128,128]{1,0:T(8,128)S(1)}) custom-call(bf16[1,128,1024]{2,1,0:T(8,128)(2,1)} %g_hbm.1, f32[1,128,1024]{2,1,0:T(8,128)} %e_hbm.1, s32[128,1024]{1,0:T(8,128)} %f_hbm.1, s32[1,128]{1,0:T(1,128)} %bitcast.2, ...), custom_call_target="tpu_custom_call" | custom-call | tf_op jit(solution)/shard_map/pallas_call | solution.py:257
  38.6 1.1 %shard_map.69 = (f32[1,128,1024]{2,1,0:T(8,128)}, f32[128,1024]{1,0:T(8,128)}) custom-call(bf16[128,1024]{1,0:T(8,128)(2,1)S(1)} %get-tuple-element.7.gathered, f32[128,1024]{1,0:T(8,128)S(1)} %get-tuple-element.8.err, s32[128,1024]{1,0:T(8,128)S(1)} %get-tuple-element.9.f, bf16[256,256]{1,0:T(8,128)(2,1)S(1)} %get-tuple-element.10.matrix, ...), custom_call_target="tpu_custom_call" | custom-call | tf_op jit(solution)/shard_map/pallas_call | solution.py:278

commit v3 on v0

v3 whole, which is shorter than its diff:
```python
import jax
import jax.numpy as jnp
from jax import lax
from jax.experimental import pallas as pl
from jax.experimental.pallas import tpu as pltpu
from jax.sharding import PartitionSpec as P

LENGTH = 1024
BLOCKS = 128
HALF = 64
XS = 8
ZS = 4
ROWS = 16
COLS = 512
LANES = 128
FACTOR = 256
PARTS = LENGTH // FACTOR
MESH = pl.DeviceIdType.MESH
CHUNK = 32
CHUNK_SLABS = ((0, 1, 5, 4), (7, 2, 6, 3))
EARLY_FIRST = (0, 1, 7, 2, 6, 3, 5, 4)
NEAR_FIRST = (0, 1, 7, 2, 6, 3, 5, 4)


def small_hadamard():
    i = lax.broadcasted_iota(jnp.int32, (FACTOR, FACTOR), 0)
    j = lax.broadcasted_iota(jnp.int32, (FACTOR, FACTOR), 1)
    bits = i & j
    bits = bits ^ (bits >> 4)
    bits = bits ^ (bits >> 2)
    bits = bits ^ (bits >> 1)
    return jnp.where((bits & 1) == 1, -1.0 / 32.0, 1.0 / 32.0).astype(jnp.bfloat16)


def rotate(x, matrix):
    rows = x.shape[0]
    stacked = jnp.concatenate(
        [x[:, part * FACTOR : (part + 1) * FACTOR] for part in range(PARTS)], axis=0
    )
    product = jnp.dot(stacked, matrix, preferred_element_type=jnp.float32)
    a, b, c, d = [product[part * rows : (part + 1) * rows] for part in range(PARTS)]
    ab, amb, cd, cmd = a + b, a - b, c + d, c - d
    return jnp.concatenate([ab + cd, amb + cmd, ab - cd, amb - cmd], axis=1)


def columns_of(row1, row2):
    both = jnp.broadcast_to((row1 + 64 * row2).astype(jnp.float32), (BLOCKS, BLOCKS))
    i = lax.broadcasted_iota(jnp.int32, (BLOCKS, BLOCKS), 0)
    j = lax.broadcasted_iota(jnp.int32, (BLOCKS, BLOCKS), 1)
    column = jnp.sum(jnp.where(i == j, both, 0.0), axis=1, keepdims=True)
    packed = jnp.broadcast_to(column, (BLOCKS, LANES)).astype(jnp.int32)
    second = (packed + 32) >> 6
    return packed - 64 * second, second


def power_two(exponents):
    return (1 << (exponents + 16)).astype(jnp.float32) * jnp.float32(2.0**-16)


def wide(scale, columns):
    return jnp.concatenate([scale] * (columns // LANES), axis=1)


def reduce_kernel(
    g_hbm, e_hbm, f_hbm, exp1_hbm, exp2_hbm, err, upd,
    g, e, f, codes, from_sibling, sums, parts, passed, gathered, matrix, exp1, exp2, up1, down1, ratio, up2,
    exp_sems, in_sems, pair_send, pair_recv, a_send, a_recv, p_send, x_send, x_recv, c_send, c_recv,
):
    me = lax.axis_index("rep")
    core = lax.rem(me, 2)
    chip = me // 2
    x, z = chip // ZS, lax.rem(chip, ZS)
    sibling = me + 1 - 2 * core
    moved = lax.axis_index("tp") == 0
    late = moved & (x == 0) & (z == 0) & (core == 0)
    owns = (z == 0) & jnp.logical_not(late)
    owns_more = moved & (x == 0) & (z == 0) & (core == 1)
    elsewhere = moved & (core == 0)

    def device(px, pz, at_core=core):
        return {"rep": (px * ZS + pz) * 2 + at_core}

    def rows_at(first_row, count):
        return pl.ds(pl.multiple_of(first_row, ROWS), count)

    def slab(s, first_row):
        return (
            rows_at(first_row + lax.rem(s, XS // 2) * ROWS, ROWS),
            pl.ds(pl.multiple_of((s // (XS // 2)) * COLS, COLS), COLS),
        )

    mine, other = core * HALF, (1 - core) * HALF

    small_loads = [
        pltpu.make_async_copy(exp1_hbm, exp1, exp_sems.at[0]),
        pltpu.make_async_copy(exp2_hbm, exp2, exp_sems.at[1]),
    ]
    for copy in small_loads:
        copy.start()
    loads = {}
    for at, (base, chunk) in enumerate(((other, 0), (other, 1), (mine, 0), (mine, 1))):
        rows = rows_at(base + chunk * CHUNK, CHUNK)
        for which, (source, target) in enumerate(((g_hbm.at[0], g), (f_hbm, f), (e_hbm.at[0], e))):
            copy = pltpu.make_async_copy(
                source.at[rows, :], target.at[rows, :], in_sems.at[3 * at + which]
            )
            copy.start()
            loads[at, which] = copy

    barrier = pltpu.get_barrier_semaphore()
    pl.semaphore_signal(barrier, inc=1, device_id={"rep": sibling}, device_id_type=MESH)

    def greet(at_core):
        @pl.loop(1, XS)
        def _(step):
            pl.semaphore_signal(
                barrier, inc=1, device_id=device(lax.rem(x + step, XS), 0, at_core),
                device_id_type=MESH,
            )

        @pl.loop(0, 2 * XS)
        def _(step):
            pl.semaphore_signal(
                barrier, inc=1, device_id=device(lax.rem(x + step // 2, XS), 1 + 2 * lax.rem(step, 2), at_core),
                device_id_type=MESH,
            )

    pl.when(owns)(lambda: greet(core))
    pl.when(owns_more)(lambda: greet(0))

    @pl.when(z == 1)
    def _():
        @pl.loop(0, XS)
        def _(step):
            pl.semaphore_signal(
                barrier, inc=1, device_id=device(lax.rem(x + step, XS), 2), device_id_type=MESH
            )

    matrix[...] = small_hadamard()
    for copy in small_loads:
        copy.wait()
    exponent1, exponent2 = columns_of(exp1[...], exp2[...])
    scale1 = power_two(exponent1)
    up1[...] = scale1
    down1[...] = power_two(-exponent1)

    def first(at, first_row):
        rows = rows_at(first_row, CHUNK)
        for which in range(3):
            loads[at, which].wait()
        signs = f[rows, :].astype(jnp.float32)
        flipped = (g[rows, :].astype(jnp.float32) * signs).astype(jnp.bfloat16)
        rotated = rotate(flipped, matrix[...]) + e[rows, :]
        code = jnp.clip(rotated * wide(down1[rows, :], LENGTH), -448.0, 448.0).astype(jnp.bfloat16)
        err[rows, :] = rotated - code.astype(jnp.float32) * wide(up1[rows, :], LENGTH)
        codes[rows, :] = code

    to_sibling = []
    for chunk in range(2):
        first(chunk, other + chunk * CHUNK)
        if chunk == 0:
            pl.semaphore_wait(barrier, jnp.where(z == 0, XS, XS + 1))
        to_sibling.append(pltpu.make_async_remote_copy(
            src_ref=codes.at[rows_at(other + chunk * CHUNK, CHUNK), :],
            dst_ref=from_sibling.at[pl.ds(chunk * CHUNK, CHUNK), :],
            send_sem=pair_send.at[chunk], recv_sem=pair_recv.at[chunk],
            device_id={"rep": sibling}, device_id_type=MESH,
        ))
        to_sibling[-1].start()
    for chunk in range(2):
        first(2 + chunk, mine + chunk * CHUNK)

    def to_owner(s):
        away = (elsewhere & (s == 0)).astype(jnp.int32)
        buffer = jnp.where(z == 2, 0, away)
        pltpu.make_async_remote_copy(
            src_ref=sums.at[slab(s, 0)], dst_ref=parts.at[buffer, z, x],
            send_sem=a_send, recv_sem=a_recv.at[buffer, z],
            device_id=device(s, jnp.where(z == 2, 1, 0), core + buffer), device_id_type=MESH,
        ).start()

    for chunk in range(2):
        to_sibling[chunk].wait()
        rows = pl.ds(chunk * CHUNK, CHUNK)
        pair = codes[rows_at(mine + chunk * CHUNK, CHUNK), :].astype(jnp.float32)
        sums[rows, :] = (pair + from_sibling[rows, :].astype(jnp.float32)).astype(jnp.bfloat16)
        for s in CHUNK_SLABS[chunk]:
            pl.when(jnp.logical_not(owns & (x == s)))(lambda s=s: to_owner(s))

    ratio[...] = scale1 * power_two(-exponent2)
    up2[...] = power_two(exponent2)

    def plane_sum(total, buffer, plane, count):
        for column in range(count):
            total = total + parts[buffer, plane, column].astype(jnp.float32)
        return total

    def slots(count):
        return parts.at[0, 0, pl.ds(0, count)]

    def wait_for(landed, sem):
        pltpu.make_async_copy(landed, landed, sem).wait()

    @pl.when(z == 1)
    def _():
        wait_for(parts.at[0, 2], a_recv.at[0, 2])
        total = plane_sum(jnp.zeros((ROWS, COLS), jnp.float32), 0, 2, XS)
        passed[...] = total.astype(jnp.bfloat16)
        buffer = (elsewhere & (x == 0)).astype(jnp.int32)
        pltpu.make_async_remote_copy(
            src_ref=passed, dst_ref=parts.at[buffer, 2, 0],
            send_sem=p_send, recv_sem=a_recv.at[buffer, 2],
            device_id=device(x, 0, core + buffer), device_id_type=MESH,
        ).start()

    def send_slab(s, at, device_id):
        own = slab(s, at)
        pltpu.make_async_remote_copy(
            src_ref=gathered.at[own], dst_ref=gathered.at[own],
            send_sem=x_send, recv_sem=x_recv.at[s],
            device_id=device_id, device_id_type=MESH,
        ).start()

    def to_row(s):
        for px in EARLY_FIRST:
            pl.when(px != x)(lambda px=px: send_slab(s, mine, device(px, z)))

    def own_slab(s, buffer, at):
        own = slab(s, at)
        total = jnp.zeros((ROWS, COLS), jnp.float32)
        for plane in range(ZS):
            if plane == 0:
                wait_for(slots(XS - 1 + buffer), a_recv.at[buffer, 0])
            elif plane == 2:
                wait_for(slots(1), a_recv.at[buffer, 2])
            else:
                wait_for(slots(XS), a_recv.at[buffer, plane])
            total = plane_sum(total, buffer, plane, 1 if plane == 2 else XS)
        scaled = total * wide(ratio[own[0], :], COLS)
        gathered[own] = jnp.clip(scaled, -448.0, 448.0).astype(jnp.bfloat16)

    def wait_slab(s):
        own = slab(s, mine)
        pltpu.make_async_copy(gathered.at[own], gathered.at[own], x_recv.at[s]).wait()

    def to_other_core(s):
        own = slab(s, mine)
        pltpu.make_async_remote_copy(
            src_ref=gathered.at[own], dst_ref=gathered.at[own],
            send_sem=c_send, recv_sem=c_recv.at[s],
            device_id={"rep": sibling}, device_id_type=MESH,
        ).start()

    @pl.when(owns)
    def _():
        parts[0, 0, x] = sums[slab(x, 0)]
        own_slab(x, 0, mine)
        send_slab(x, mine, device(x, 1))
        to_row(x)
        send_slab(x, mine, device(x, 2))
        send_slab(x, mine, device(x, 3))

    @pl.when(owns_more)
    def _():
        own_slab(0, 1, 0)
        send_slab(0, 0, device(0, 1, 0))
        for px in EARLY_FIRST:
            send_slab(0, 0, device(px, 0, 0))
        send_slab(0, 0, device(0, 2, 0))
        send_slab(0, 0, device(0, 3, 0))

    @pl.when(z != 0)
    def _():
        wait_slab(x)
        to_row(x)

    for step in NEAR_FIRST:
        s = lax.rem(x + step, XS)
        if step == 0:
            pl.when(late)(lambda: wait_slab(x))
            pl.when(jnp.logical_not(late))(lambda: to_other_core(x))
        else:
            wait_slab(s)
            to_other_core(s)

    def last(rows):
        restored = rotate(gathered[rows, :], matrix[...]) * wide(up2[rows, :], LENGTH)
        upd[rows, :] = restored * f[rows, :].astype(jnp.float32)

    last(rows_at(mine, HALF))
    for group in range(XS // 2):
        for s in (group, group + XS // 2):
            held = owns_more & (s == 0)
            pl.when(jnp.logical_not(held))(lambda s=s: wait_for(slots(1), c_recv.at[s]))
        last(rows_at(other + group * ROWS, ROWS))

    @pl.when(owns)
    def _():
        wait_for(slots(XS - 1), a_send)
        wait_for(parts.at[0, pl.ds(0, 2), pl.ds(0, 5)], x_send)

    @pl.when(owns_more)
    def _():
        wait_for(slots(XS), x_send)
        wait_for(slots(3), x_send)

    @pl.when(jnp.logical_not(owns))
    def _():
        wait_for(slots(XS), a_send)

    @pl.when(z != 0)
    def _():
        wait_for(slots(XS - 1), x_send)

    @pl.when(z == 1)
    def _():
        wait_for(passed, p_send)

    wait_for(slots(XS - 1), c_send)
    pl.when(jnp.logical_not(late))(lambda: wait_for(slots(1), c_send))


def write_kernel(err, upd, err_hbm, upd_hbm, out_sems):
    stores = []
    for at in range(BLOCKS // CHUNK):
        rows = pl.ds(at * CHUNK, CHUNK)
        for which, (source, target) in enumerate(((err, err_hbm.at[0]), (upd, upd_hbm))):
            copy = pltpu.make_async_copy(
                source.at[rows, :], target.at[rows, :], out_sems.at[2 * at + which]
            )
            copy.start()
            stores.append(copy)
    for copy in stores:
        copy.wait()


def per_device(gradients, errors, sign_flips, first_exponents, second_exponents):
    hbm = pl.BlockSpec(memory_space=pl.ANY)
    vmem = pl.BlockSpec(memory_space=pltpu.VMEM)
    whole = (BLOCKS, LENGTH)
    f32, bf16, i32 = jnp.float32, jnp.bfloat16, jnp.int32
    dma = pltpu.SemaphoreType.DMA
    scale = pltpu.VMEM((BLOCKS, LANES), f32)
    arguments = (
        gradients, errors, sign_flips,
        first_exponents.reshape(1, BLOCKS), second_exponents.reshape(1, BLOCKS),
    )
    held = pl.pallas_call(
        reduce_kernel,
        out_shape=(pltpu.VMEM(whole, f32), pltpu.VMEM(whole, f32)),
        in_specs=[hbm] * 5,
        out_specs=(vmem, vmem),
        scratch_shapes=[
            pltpu.VMEM(whole, bf16), pltpu.VMEM(whole, f32), pltpu.VMEM(whole, i32),
            pltpu.VMEM(whole, bf16), pltpu.VMEM((HALF, LENGTH), bf16), pltpu.VMEM((HALF, LENGTH), bf16),
            pltpu.VMEM((2, ZS, XS, ROWS, COLS), bf16), pltpu.VMEM((ROWS, COLS), bf16),
            pltpu.VMEM(whole, bf16),
            pltpu.VMEM((FACTOR, FACTOR), bf16),
            pltpu.VMEM((1, BLOCKS), i32), pltpu.VMEM((1, BLOCKS), i32), scale, scale, scale, scale,
            dma((2,)), dma((12,)), dma((2,)), dma((2,)), dma, dma((2, ZS)), dma, dma, dma((XS,)),
            dma, dma((XS,)),
        ],
        compiler_params=pltpu.CompilerParams(
            collective_id=0, has_side_effects=True, vmem_limit_bytes=16 * 2**20
        ),
    )(*[pltpu.with_memory_space_constraint(array, pltpu.HBM) for array in arguments])
    return pl.pallas_call(
        write_kernel,
        out_shape=(jax.ShapeDtypeStruct((1, *whole), f32), jax.ShapeDtypeStruct(whole, f32)),
        in_specs=[vmem, vmem],
        out_specs=(hbm, hbm),
        scratch_shapes=[dma((2 * BLOCKS // CHUNK,))],
        compiler_params=pltpu.CompilerParams(vmem_limit_bytes=16 * 2**20),
    )(*held)


def solution(mesh):
    in_specs = (P("rep", "tp", None), P("rep", "tp", None), P("tp", None), P("tp"), P("tp"))
    out_specs = (P("rep", "tp", None), P("tp", None))
    return jax.shard_map(
        per_device, mesh=mesh, in_specs=in_specs, out_specs=out_specs, check_vma=False
    )
```

time: 689 us -> 37.3 us (0.05)
  waiting for transfers between devices: 571 us -> 0 us
  blocking collectives: 82.4 us -> 0 us
  Pallas kernels: 0 us -> 36.5 us
  matrix products: 17.8 us -> 0 us
  between operations: 14.7 us -> 0.64 us
    unnamed x2 -> x0, waiting for transfers between devices: 571 us -> none
    all_gather x1 -> x0, blocking collectives: 82.4 us -> none  [per_device(): lax.all_gather(second_codes, 'rep', axis=0, tiled=True).astype(jnp.float32)]
    pallas_call x0 -> x2, Pallas kernels: none -> 36.5 us  [the longest x1 35.5 us: per_device(): pl.pallas_call(reduce_kernel, out_shape=(pltpu.VMEM(whole, f32), pltpu.VM...]
    dot_general x2 -> x0, matrix products: 17.8 us -> none  [the longest x1 9.59 us: per_device(): jnp.dot(flipped, hadamard, precision=lax.Precision.HIGHEST) + errors[0]]
  transfers between devices with their start and end apart: 1 -> 0, of which waited for: 1 -> 0; matrix products, arithmetic and copies ran while one was open for 0% -> 0% of each run, Pallas kernels for 0% -> 0%
where the time goes in v3:
time: 37.3 us; the launch traced here: 37.1 us
  Pallas kernels  36.5 us (98%)
  between operations  0.64 us (2%)
    pallas_call x1, Pallas kernels, per_device(): pl.pallas_call(reduce_kernel, out_shape=(pltpu.VMEM(whole, f32), pltpu.VM...  35.5 us
    pallas_call x1, Pallas kernels, per_device(): pl.pallas_call(write_kernel, out_shape=(jax.ShapeDtypeStruct((1, *whole),...  1.03 us

profile of v3, /device:TPU:1, one launch (start us, length us, event | category | flops | bytes accessed | tf_op | source)
XLA Modules:
  0.0 37.1 jit_solution(9191382427390502360)
XLA Ops:
  0.6 35.5 %shard_map.68 = (f32[128,1024]{1,0:T(8,128)S(1)}, f32[128,1024]{1,0:T(8,128)S(1)}) custom-call(bf16[1,128,1024]{2,1,0:T(8,128)(2,1)} %g_hbm.1, f32[1,128,1024]{2,1,0:T(8,128)} %e_hbm.1, s32[128,1024]{1,0:T(8,128)} %f_hbm.1, s32[1,128]{1,0:T(1,128)} %bitcast.2, s32[1,128]{1,0:T(1,128)} %bitcast.3), custom_call_target="tpu_custom_call" | custom-call | tf_op jit(solution)/shard_map/pallas_call | solution.py:348
  36.1 1.0 %shard_map.69 = (f32[1,128,1024]{2,1,0:T(8,128)}, f32[128,1024]{1,0:T(8,128)}) custom-call(f32[128,1024]{1,0:T(8,128)S(1)} %get-tuple-element.4.err, f32[128,1024]{1,0:T(8,128)S(1)} %get-tuple-element.5.upd), custom_call_target="tpu_custom_call" | custom-call | tf_op jit(solution)/shard_map/pallas_call | solution.py:367

commit v4 on v3

--- a/solution.py
+++ b/solution.py
@@ -11,15 +11,21 @@
 XS = 8
 ZS = 4
 ROWS = 16
-COLS = 512
+UNIT = 256
+COLS = 768
 LANES = 128
 FACTOR = 256
 PARTS = LENGTH // FACTOR
 MESH = pl.DeviceIdType.MESH
 CHUNK = 32
-CHUNK_SLABS = ((0, 1, 5, 4), (7, 2, 6, 3))
+CHUNK_SLABS = ((4, 0, 3, 5), (2, 6, 1, 7))
+SLABS = (
+    (0, 0, 768), (48, 0, 512), (32, 0, 512), (16, 0, 512),
+    (0, 768, 256), (16, 512, 512), (32, 512, 512), (48, 512, 512),
+)
+WIDTHS = (256, 512, 768)
 EARLY_FIRST = (0, 1, 7, 2, 6, 3, 5, 4)
-NEAR_FIRST = (0, 1, 7, 2, 6, 3, 5, 4)
+PAIRS = XS // 2
 
 
 def small_hadamard():
@@ -84,12 +90,34 @@
         return pl.ds(pl.multiple_of(first_row, ROWS), count)
 
     def slab(s, first_row):
+        if isinstance(s, int):
+            row, column, width = SLABS[s]
+            return rows_at(first_row + row, ROWS), pl.ds(column, width)
+        index, width = s
+        row, column = jnp.int32(0), jnp.int32(0)
+        for at, (own_row, own_column, own_width) in enumerate(SLABS):
+            if own_width == width:
+                row = jnp.where(index == at, own_row, row)
+                column = jnp.where(index == at, own_column, column)
         return (
-            rows_at(first_row + lax.rem(s, XS // 2) * ROWS, ROWS),
-            pl.ds(pl.multiple_of((s // (XS // 2)) * COLS, COLS), COLS),
+            rows_at(first_row + row, ROWS),
+            pl.ds(pl.multiple_of(column, UNIT), width),
         )
 
+    def width_of(s):
+        return SLABS[s][2] if isinstance(s, int) else s[1]
+
+    def index_of(s):
+        return s if isinstance(s, int) else s[0]
+
+    def of_own_width(condition, work):
+        for width in WIDTHS:
+            fits = jnp.where(x == 0, 768, jnp.where(x == XS // 2, 256, 512)) == width
+            pl.when(condition & fits)(lambda width=width: work((x, width)))
+
     mine, other = core * HALF, (1 - core) * HALF
+    def chunk_at(base, turn):
+        return rows_at(base + turn * CHUNK, CHUNK)
 
     small_loads = [
         pltpu.make_async_copy(exp1_hbm, exp1, exp_sems.at[0]),
@@ -98,8 +126,8 @@
     for copy in small_loads:
         copy.start()
     loads = {}
-    for at, (base, chunk) in enumerate(((other, 0), (other, 1), (mine, 0), (mine, 1))):
-        rows = rows_at(base + chunk * CHUNK, CHUNK)
+    for at, (base, turn) in enumerate(((other, 0), (other, 1), (mine, 0), (mine, 1))):
+        rows = chunk_at(base, turn)
         for which, (source, target) in enumerate(((g_hbm.at[0], g), (f_hbm, f), (e_hbm.at[0], e))):
             copy = pltpu.make_async_copy(
                 source.at[rows, :], target.at[rows, :], in_sems.at[3 * at + which]
@@ -144,8 +172,7 @@
     up1[...] = scale1
     down1[...] = power_two(-exponent1)
 
-    def first(at, first_row):
-        rows = rows_at(first_row, CHUNK)
+    def first(at, rows):
         for which in range(3):
             loads[at, which].wait()
         signs = f[rows, :].astype(jnp.float32)
@@ -157,34 +184,36 @@
 
     to_sibling = []
     for chunk in range(2):
-        first(chunk, other + chunk * CHUNK)
+        first(chunk, chunk_at(other, chunk))
         if chunk == 0:
             pl.semaphore_wait(barrier, jnp.where(z == 0, XS, XS + 1))
         to_sibling.append(pltpu.make_async_remote_copy(
-            src_ref=codes.at[rows_at(other + chunk * CHUNK, CHUNK), :],
-            dst_ref=from_sibling.at[pl.ds(chunk * CHUNK, CHUNK), :],
+            src_ref=codes.at[chunk_at(other, chunk), :],
+            dst_ref=from_sibling.at[chunk_at(0, chunk), :],
             send_sem=pair_send.at[chunk], recv_sem=pair_recv.at[chunk],
             device_id={"rep": sibling}, device_id_type=MESH,
         ))
         to_sibling[-1].start()
     for chunk in range(2):
-        first(2 + chunk, mine + chunk * CHUNK)
+        first(2 + chunk, chunk_at(mine, chunk))
 
     def to_owner(s):
         away = (elsewhere & (s == 0)).astype(jnp.int32)
-        buffer = jnp.where(z == 2, 0, away)
+        to_pass = z == 2
+        buffer = jnp.where(to_pass, 0, away)
         pltpu.make_async_remote_copy(
-            src_ref=sums.at[slab(s, 0)], dst_ref=parts.at[buffer, z, x],
+            src_ref=sums.at[slab(s, 0)], dst_ref=parts.at[buffer, z, x, :, pl.ds(0, width_of(s))],
             send_sem=a_send, recv_sem=a_recv.at[buffer, z],
-            device_id=device(s, jnp.where(z == 2, 1, 0), core + buffer), device_id_type=MESH,
+            device_id=device(s, jnp.where(to_pass, 1, 0), core + buffer), device_id_type=MESH,
         ).start()
 
     for chunk in range(2):
         to_sibling[chunk].wait()
-        rows = pl.ds(chunk * CHUNK, CHUNK)
-        pair = codes[rows_at(mine + chunk * CHUNK, CHUNK), :].astype(jnp.float32)
+        rows = chunk_at(0, chunk)
+        pair = codes[chunk_at(mine, chunk), :].astype(jnp.float32)
         sums[rows, :] = (pair + from_sibling[rows, :].astype(jnp.float32)).astype(jnp.bfloat16)
-        for s in CHUNK_SLABS[chunk]:
+        for turn in range(XS // 2):
+            s = CHUNK_SLABS[chunk][turn]
             pl.when(jnp.logical_not(owns & (x == s)))(lambda s=s: to_owner(s))
 
     ratio[...] = scale1 * power_two(-exponent2)
@@ -192,32 +221,36 @@
 
     def plane_sum(total, buffer, plane, count):
         for column in range(count):
-            total = total + parts[buffer, plane, column].astype(jnp.float32)
+            part = parts[buffer, plane, column, :, pl.ds(0, total.shape[1])]
+            total = total + part.astype(jnp.float32)
         return total
 
-    def slots(count):
-        return parts.at[0, 0, pl.ds(0, count)]
+    def slots(count, width):
+        return parts.at[0, 0, pl.ds(0, count), :, pl.ds(0, width)]
 
     def wait_for(landed, sem):
         pltpu.make_async_copy(landed, landed, sem).wait()
 
-    @pl.when(z == 1)
-    def _():
-        wait_for(parts.at[0, 2], a_recv.at[0, 2])
-        total = plane_sum(jnp.zeros((ROWS, COLS), jnp.float32), 0, 2, XS)
-        passed[...] = total.astype(jnp.bfloat16)
+    def pass_on(s):
+        width = width_of(s)
+        wait_for(slots(XS, width), a_recv.at[0, 2])
+        total = plane_sum(jnp.zeros((ROWS, width), jnp.float32), 0, 2, XS)
+        staged = passed.at[:, pl.ds(0, width)]
+        staged[...] = total.astype(jnp.bfloat16)
         buffer = (elsewhere & (x == 0)).astype(jnp.int32)
         pltpu.make_async_remote_copy(
-            src_ref=passed, dst_ref=parts.at[buffer, 2, 0],
+            src_ref=staged, dst_ref=parts.at[buffer, 2, 0, :, pl.ds(0, width)],
             send_sem=p_send, recv_sem=a_recv.at[buffer, 2],
             device_id=device(x, 0, core + buffer), device_id_type=MESH,
         ).start()
+
+    of_own_width(z == 1, pass_on)
 
     def send_slab(s, at, device_id):
         own = slab(s, at)
         pltpu.make_async_remote_copy(
             src_ref=gathered.at[own], dst_ref=gathered.at[own],
-            send_sem=x_send, recv_sem=x_recv.at[s],
+            send_sem=x_send, recv_sem=x_recv.at[index_of(s)],
             device_id=device_id, device_id_type=MESH,
         ).start()
 
@@ -226,39 +259,40 @@
             pl.when(px != x)(lambda px=px: send_slab(s, mine, device(px, z)))
 
     def own_slab(s, buffer, at):
-        own = slab(s, at)
-        total = jnp.zeros((ROWS, COLS), jnp.float32)
-        for plane in range(ZS):
+        own, width = slab(s, at), width_of(s)
+        total = jnp.zeros((ROWS, width), jnp.float32)
+        for plane in (0, 1, 3, 2):
             if plane == 0:
-                wait_for(slots(XS - 1 + buffer), a_recv.at[buffer, 0])
+                wait_for(slots(XS - 1 + buffer, width), a_recv.at[buffer, 0])
             elif plane == 2:
-                wait_for(slots(1), a_recv.at[buffer, 2])
+                wait_for(slots(1, width), a_recv.at[buffer, 2])
             else:
-                wait_for(slots(XS), a_recv.at[buffer, plane])
+                wait_for(slots(XS, width), a_recv.at[buffer, plane])
             total = plane_sum(total, buffer, plane, 1 if plane == 2 else XS)
-        scaled = total * wide(ratio[own[0], :], COLS)
+        scaled = total * wide(ratio[own[0], :], width)
         gathered[own] = jnp.clip(scaled, -448.0, 448.0).astype(jnp.bfloat16)
 
     def wait_slab(s):
         own = slab(s, mine)
-        pltpu.make_async_copy(gathered.at[own], gathered.at[own], x_recv.at[s]).wait()
+        wait_for(gathered.at[own], x_recv.at[index_of(s)])
 
     def to_other_core(s):
         own = slab(s, mine)
         pltpu.make_async_remote_copy(
             src_ref=gathered.at[own], dst_ref=gathered.at[own],
-            send_sem=c_send, recv_sem=c_recv.at[s],
+            send_sem=c_send, recv_sem=c_recv.at[index_of(s)],
             device_id={"rep": sibling}, device_id_type=MESH,
         ).start()
 
-    @pl.when(owns)
-    def _():
-        parts[0, 0, x] = sums[slab(x, 0)]
-        own_slab(x, 0, mine)
-        send_slab(x, mine, device(x, 1))
-        to_row(x)
-        send_slab(x, mine, device(x, 2))
-        send_slab(x, mine, device(x, 3))
+    def finish(s):
+        parts[0, 0, x, :, pl.ds(0, width_of(s))] = sums[slab(s, 0)]
+        own_slab(s, 0, mine)
+        send_slab(s, mine, device(x, 1))
+        to_row(s)
+        send_slab(s, mine, device(x, 2))
+        send_slab(s, mine, device(x, 3))
+
+    of_own_width(owns, finish)
 
     @pl.when(owns_more)
     def _():
@@ -269,55 +303,63 @@
         send_slab(0, 0, device(0, 2, 0))
         send_slab(0, 0, device(0, 3, 0))
 
-    @pl.when(z != 0)
-    def _():
-        wait_slab(x)
-        to_row(x)
-
-    for step in NEAR_FIRST:
-        s = lax.rem(x + step, XS)
-        if step == 0:
-            pl.when(late)(lambda: wait_slab(x))
-            pl.when(jnp.logical_not(late))(lambda: to_other_core(x))
-        else:
-            wait_slab(s)
-            to_other_core(s)
+    def relay(s):
+        wait_slab(s)
+        to_row(s)
+
+    of_own_width(z != 0, relay)
 
     def last(rows):
         restored = rotate(gathered[rows, :], matrix[...]) * wide(up2[rows, :], LENGTH)
         upd[rows, :] = restored * f[rows, :].astype(jnp.float32)
 
+    def hand_over(order):
+        for s in order:
+            here = (s == x) & jnp.logical_not(late)
+            pl.when(jnp.logical_not(here))(lambda s=s: wait_slab(s))
+            if s == 0:
+                pl.when(jnp.logical_not(late))(lambda: to_other_core(0))
+            else:
+                to_other_core(s)
+
+    near_zero = (x < 3) | (x > 5)
+    pl.when(near_zero)(lambda: hand_over((0, 1, 7, 2, 6, 3, 5, 4)))
+    pl.when(jnp.logical_not(near_zero))(lambda: hand_over((4, 3, 5, 2, 6, 1, 7, 0)))
     last(rows_at(mine, HALF))
-    for group in range(XS // 2):
-        for s in (group, group + XS // 2):
-            held = owns_more & (s == 0)
-            pl.when(jnp.logical_not(held))(lambda s=s: wait_for(slots(1), c_recv.at[s]))
-        last(rows_at(other + group * ROWS, ROWS))
-
-    @pl.when(owns)
-    def _():
-        wait_for(slots(XS - 1), a_send)
-        wait_for(parts.at[0, pl.ds(0, 2), pl.ds(0, 5)], x_send)
-
-    @pl.when(owns_more)
-    def _():
-        wait_for(slots(XS), x_send)
-        wait_for(slots(3), x_send)
-
-    @pl.when(jnp.logical_not(owns))
-    def _():
-        wait_for(slots(XS), a_send)
-
-    @pl.when(z != 0)
-    def _():
-        wait_for(slots(XS - 1), x_send)
-
-    @pl.when(z == 1)
-    def _():
-        wait_for(passed, p_send)
-
-    wait_for(slots(XS - 1), c_send)
-    pl.when(jnp.logical_not(late))(lambda: wait_for(slots(1), c_send))
+    for s in range(XS):
+        if s == 0:
+            pl.when(jnp.logical_not(owns_more))(lambda: wait_for(slots(1, width_of(0)), c_recv.at[0]))
+        else:
+            wait_for(slots(1, width_of(s)), c_recv.at[s])
+    last(rows_at(other, HALF))
+
+    def sent(units, sem):
+        if units // 4:
+            wait_for(codes.at[pl.ds(0, ROWS * (units // 4)), :], sem)
+        if units % 4:
+            wait_for(codes.at[pl.ds(0, ROWS), pl.ds(0, UNIT * (units % 4))], sem)
+
+    def sent_all(s):
+        units = width_of(s) // UNIT
+
+        @pl.when(owns)
+        def _():
+            sent(4 * XS // 2 - units, a_send)
+            sent(10 * units, x_send)
+
+        @pl.when(z != 0)
+        def _():
+            sent((XS - 1) * units, x_send)
+
+        @pl.when(z == 1)
+        def _():
+            sent(units, p_send)
+
+    of_own_width(z >= 0, sent_all)
+    pl.when(jnp.logical_not(owns))(lambda: sent(4 * XS // 2, a_send))
+    pl.when(owns_more)(lambda: sent(11 * width_of(0) // UNIT, x_send))
+    pl.when(jnp.logical_not(late))(lambda: sent(4 * XS // 2, c_send))
+    pl.when(late)(lambda: sent(4 * XS // 2 - width_of(0) // UNIT, c_send))
 
 
 def write_kernel(err, upd, err_hbm, upd_hbm, out_sems):

time: 37.3 us -> 35.5 us (0.952); the launches traced: 37.1 us -> 34.8 us
  Pallas kernels: 36.5 us -> 34.2 us
    pallas_call x1, Pallas kernels: 35.5 us -> 33.2 us  [per_device(): pl.pallas_call(reduce_kernel, out_shape=(pltpu.VMEM(whole, f32), pltpu.VM...]
where the time goes in v4:
time: 35.5 us; the launch traced here: 34.8 us
  Pallas kernels  34.2 us (96%)
  between operations  0.64 us (2%)
    pallas_call x1, Pallas kernels, per_device(): pl.pallas_call(reduce_kernel, out_shape=(pltpu.VMEM(whole, f32), pltpu.VM...  33.2 us
    pallas_call x1, Pallas kernels, per_device(): pl.pallas_call(write_kernel, out_shape=(jax.ShapeDtypeStruct((1, *whole),...  1.03 us

profile of v4, /device:TPU:1, one launch (start us, length us, event | category | flops | bytes accessed | tf_op | source)
XLA Modules:
  0.0 34.8 jit_solution(1179568689005979861)
XLA Ops:
  0.6 33.2 %shard_map.68 = (f32[128,1024]{1,0:T(8,128)S(1)}, f32[128,1024]{1,0:T(8,128)S(1)}) custom-call(bf16[1,128,1024]{2,1,0:T(8,128)(2,1)} %g_hbm.1, f32[1,128,1024]{2,1,0:T(8,128)} %e_hbm.1, s32[128,1024]{1,0:T(8,128)} %f_hbm.1, s32[1,128]{1,0:T(1,128)} %bitcast.2, s32[1,128]{1,0:T(1,128)} %bitcast.3), custom_call_target="tpu_custom_call" | custom-call | tf_op jit(solution)/shard_map/pallas_call | solution.py:390
  33.8 1.0 %shard_map.69 = (f32[1,128,1024]{2,1,0:T(8,128)}, f32[128,1024]{1,0:T(8,128)}) custom-call(f32[128,1024]{1,0:T(8,128)S(1)} %get-tuple-element.4.err, f32[128,1024]{1,0:T(8,128)S(1)} %get-tuple-element.5.upd), custom_call_target="tpu_custom_call" | custom-call | tf_op jit(solution)/shard_map/pallas_call | solution.py:409

commit v5 on v4

--- a/solution.py
+++ b/solution.py
@@ -18,7 +18,7 @@
 PARTS = LENGTH // FACTOR
 MESH = pl.DeviceIdType.MESH
 CHUNK = 32
-CHUNK_SLABS = ((4, 0, 3, 5), (2, 6, 1, 7))
+CHUNK_SLABS = ((0, 4, 3, 5), (1, 7, 2, 6))
 SLABS = (
     (0, 0, 768), (48, 0, 512), (32, 0, 512), (16, 0, 512),
     (0, 768, 256), (16, 512, 512), (32, 512, 512), (48, 512, 512),
@@ -212,9 +212,16 @@
         rows = chunk_at(0, chunk)
         pair = codes[chunk_at(mine, chunk), :].astype(jnp.float32)
         sums[rows, :] = (pair + from_sibling[rows, :].astype(jnp.float32)).astype(jnp.bfloat16)
-        for turn in range(XS // 2):
-            s = CHUNK_SLABS[chunk][turn]
-            pl.when(jnp.logical_not(owns & (x == s)))(lambda s=s: to_owner(s))
+
+        @pl.when(z != 0)
+        def _():
+            for s in CHUNK_SLABS[chunk]:
+                to_owner(s)
+
+        @pl.when(z == 0)
+        def _():
+            for s in CHUNK_SLABS[chunk]:
+                pl.when(jnp.logical_not(owns & (x == s)))(lambda s=s: to_owner(s))
 
     ratio[...] = scale1 * power_two(-exponent2)
     up2[...] = power_two(exponent2)
@@ -255,8 +262,11 @@
         ).start()
 
     def to_row(s):
-        for px in EARLY_FIRST:
-            pl.when(px != x)(lambda px=px: send_slab(s, mine, device(px, z)))
+        reached = False
+        for at in range(XS - 1):
+            reached = (x == EARLY_FIRST[at]) | reached
+            px = jnp.where(reached, EARLY_FIRST[at + 1], EARLY_FIRST[at])
+            send_slab(s, mine, device(px, z))
 
     def own_slab(s, buffer, at):
         own, width = slab(s, at), width_of(s)

time: 35.5 us -> 35.2 us (level)
  no operation moved by 1% of the time
where the time goes in v5:
time: 35.2 us; the launch traced here: 34.8 us
  Pallas kernels  34.2 us (97%)
  between operations  0.64 us (2%)
    pallas_call x1, Pallas kernels, per_device(): pl.pallas_call(reduce_kernel, out_shape=(pltpu.VMEM(whole, f32), pltpu.VM...  33.2 us
    pallas_call x1, Pallas kernels, per_device(): pl.pallas_call(write_kernel, out_shape=(jax.ShapeDtypeStruct((1, *whole),...  1.03 us

profile of v5, /device:TPU:1, one launch (start us, length us, event | category | flops | bytes accessed | tf_op | source)
XLA Modules:
  0.0 34.8 jit_solution(5200971190149397190)
XLA Ops:
  0.6 33.2 %shard_map.68 = (f32[128,1024]{1,0:T(8,128)S(1)}, f32[128,1024]{1,0:T(8,128)S(1)}) custom-call(bf16[1,128,1024]{2,1,0:T(8,128)(2,1)} %g_hbm.1, f32[1,128,1024]{2,1,0:T(8,128)} %e_hbm.1, s32[128,1024]{1,0:T(8,128)} %f_hbm.1, s32[1,128]{1,0:T(1,128)} %bitcast.2, s32[1,128]{1,0:T(1,128)} %bitcast.3), custom_call_target="tpu_custom_call" | custom-call | tf_op jit(solution)/shard_map/pallas_call | solution.py:400
  33.8 1.0 %shard_map.69 = (f32[1,128,1024]{2,1,0:T(8,128)}, f32[128,1024]{1,0:T(8,128)}) custom-call(f32[128,1024]{1,0:T(8,128)S(1)} %get-tuple-element.4.err, f32[128,1024]{1,0:T(8,128)S(1)} %get-tuple-element.5.upd), custom_call_target="tpu_custom_call" | custom-call | tf_op jit(solution)/shard_map/pallas_call | solution.py:419

commit v6 on v5

--- a/solution.py
+++ b/solution.py
@@ -17,8 +17,9 @@
 FACTOR = 256
 PARTS = LENGTH // FACTOR
 MESH = pl.DeviceIdType.MESH
-CHUNK = 32
-CHUNK_SLABS = ((0, 4, 3, 5), (1, 7, 2, 6))
+CHUNK = 64
+CHUNKS = 1
+CHUNK_SLABS = ((0, 1, 7, 4, 2, 6, 3, 5),)
 SLABS = (
     (0, 0, 768), (48, 0, 512), (32, 0, 512), (16, 0, 512),
     (0, 768, 256), (16, 512, 512), (32, 512, 512), (48, 512, 512),
@@ -126,7 +127,8 @@
     for copy in small_loads:
         copy.start()
     loads = {}
-    for at, (base, turn) in enumerate(((other, 0), (other, 1), (mine, 0), (mine, 1))):
+    places = [(base, turn) for base in (other, mine) for turn in range(CHUNKS)]
+    for at, (base, turn) in enumerate(places):
         rows = chunk_at(base, turn)
         for which, (source, target) in enumerate(((g_hbm.at[0], g), (f_hbm, f), (e_hbm.at[0], e))):
             copy = pltpu.make_async_copy(
@@ -183,7 +185,7 @@
         codes[rows, :] = code
 
     to_sibling = []
-    for chunk in range(2):
+    for chunk in range(CHUNKS):
         first(chunk, chunk_at(other, chunk))
         if chunk == 0:
             pl.semaphore_wait(barrier, jnp.where(z == 0, XS, XS + 1))
@@ -194,8 +196,8 @@
             device_id={"rep": sibling}, device_id_type=MESH,
         ))
         to_sibling[-1].start()
-    for chunk in range(2):
-        first(2 + chunk, chunk_at(mine, chunk))
+    for chunk in range(CHUNKS):
+        first(CHUNKS + chunk, chunk_at(mine, chunk))
 
     def to_owner(s):
         away = (elsewhere & (s == 0)).astype(jnp.int32)
@@ -207,7 +209,7 @@
             device_id=device(s, jnp.where(to_pass, 1, 0), core + buffer), device_id_type=MESH,
         ).start()
 
-    for chunk in range(2):
+    for chunk in range(CHUNKS):
         to_sibling[chunk].wait()
         rows = chunk_at(0, chunk)
         pair = codes[chunk_at(mine, chunk), :].astype(jnp.float32)
@@ -374,8 +376,8 @@
 
 def write_kernel(err, upd, err_hbm, upd_hbm, out_sems):
     stores = []
-    for at in range(BLOCKS // CHUNK):
-        rows = pl.ds(at * CHUNK, CHUNK)
+    for at in range(BLOCKS // 32):
+        rows = pl.ds(at * 32, 32)
         for which, (source, target) in enumerate(((err, err_hbm.at[0]), (upd, upd_hbm))):
             copy = pltpu.make_async_copy(
                 source.at[rows, :], target.at[rows, :], out_sems.at[2 * at + which]
@@ -409,7 +411,7 @@
             pltpu.VMEM(whole, bf16),
             pltpu.VMEM((FACTOR, FACTOR), bf16),
             pltpu.VMEM((1, BLOCKS), i32), pltpu.VMEM((1, BLOCKS), i32), scale, scale, scale, scale,
-            dma((2,)), dma((12,)), dma((2,)), dma((2,)), dma, dma((2, ZS)), dma, dma, dma((XS,)),
+            dma((2,)), dma((6 * CHUNKS,)), dma((CHUNKS,)), dma((CHUNKS,)), dma, dma((2, ZS)), dma, dma, dma((XS,)),
             dma, dma((XS,)),
         ],
         compiler_params=pltpu.CompilerParams(
@@ -421,7 +423,7 @@
         out_shape=(jax.ShapeDtypeStruct((1, *whole), f32), jax.ShapeDtypeStruct(whole, f32)),
         in_specs=[vmem, vmem],
         out_specs=(hbm, hbm),
-        scratch_shapes=[dma((2 * BLOCKS // CHUNK,))],
+        scratch_shapes=[dma((2 * BLOCKS // 32,))],
         compiler_params=pltpu.CompilerParams(vmem_limit_bytes=16 * 2**20),
     )(*held)
 

time: 35.2 us -> 35.2 us (level)
  no operation moved by 1% of the time
where the time goes in v6:
time: 35.2 us; the launch traced here: 35 us
  Pallas kernels  34.4 us (98%)
  between operations  0.64 us (2%)
    pallas_call x1, Pallas kernels, per_device(): pl.pallas_call(reduce_kernel, out_shape=(pltpu.VMEM(whole, f32), pltpu.VM...  33.3 us
    pallas_call x1, Pallas kernels, per_device(): pl.pallas_call(write_kernel, out_shape=(jax.ShapeDtypeStruct((1, *whole),...  1.03 us

profile of v6, /device:TPU:1, one launch (start us, length us, event | category | flops | bytes accessed | tf_op | source)
XLA Modules:
  0.0 35.0 jit_solution(2513467958491596090)
XLA Ops:
  0.6 33.3 %shard_map.68 = (f32[128,1024]{1,0:T(8,128)S(1)}, f32[128,1024]{1,0:T(8,128)S(1)}) custom-call(bf16[1,128,1024]{2,1,0:T(8,128)(2,1)} %g_hbm.1, f32[1,128,1024]{2,1,0:T(8,128)} %e_hbm.1, s32[128,1024]{1,0:T(8,128)} %f_hbm.1, s32[1,128]{1,0:T(1,128)} %bitcast.2, s32[1,128]{1,0:T(1,128)} %bitcast.3), custom_call_target="tpu_custom_call" | custom-call | tf_op jit(solution)/shard_map/pallas_call | solution.py:402
  34.0 1.0 %shard_map.69 = (f32[1,128,1024]{2,1,0:T(8,128)}, f32[128,1024]{1,0:T(8,128)}) custom-call(f32[128,1024]{1,0:T(8,128)S(1)} %get-tuple-element.4.err, f32[128,1024]{1,0:T(8,128)S(1)} %get-tuple-element.5.upd), custom_call_target="tpu_custom_call" | custom-call | tf_op jit(solution)/shard_map/pallas_call | solution.py:421
